TPU v7x, 128 devices: a whole 4x4x4 slice. The times are simulated.
128 devices in a mesh: row: 8 (over y_lo, z), stop: 16 (over y_hi, x, core).
Axes of the slice: x: 4, y: 4 (y_hi: 2, y_lo: 2; y = y_hi * 2 + y_lo), z: 4, core: 2. Of those that a mesh axis runs over, the one named last changes fastest.
Arguments:
- radiosity: bfloat16 [32, 1024, 256], P('row', 'stop'), may hold values from -6 to 6
- emission: bfloat16 [32, 1024, 256], P('row', 'stop'), may hold values from -6 to 6
- areas: float32 [32, 1024], P('row', 'stop'), may hold values from 0.25 to 4
- patch_material: int32 [32, 1024], P('row', 'stop'), may hold values from 0 to 15
- reflect_table: float32 [16, 32], replicated, may hold values from 0.2 to 0.95
- pair_blocks: bfloat16 [32, 16, 1024, 1024], P('row', 'stop'), may hold values from 0.0005493164 to 0.016479492
- far_blocks: bfloat16 [32, 1024, 1024], P('row', 'stop'), may hold values from 0.0005493164 to 0.016479492
Outputs:
- updated: float32 [32, 1024, 256], P('row', 'stop')
All inputs are finite; a program needn't handle non-finite values.
Results may differ from a plain program's by a relative error of at most 0.0003.
Values may be sent and summed in bfloat16 or wider, within the bound.
A program may use at most 192 MiB of HBM per device.

v0:
```python
import jax
import jax.numpy as jnp
from jax import lax
from jax.sharding import PartitionSpec as P


def shifted(shard, axis, by):
    peers = lax.axis_size(axis)
    return lax.ppermute(shard, axis, [(i, (i + by) % peers) for i in range(peers)])


def on_device(radiosity, emission, areas, patch_material, reflect_table, pair_blocks, far_blocks):
    reach = lax.axis_size("row") // 2
    stop_index = lax.axis_index("stop")
    per_row = radiosity.shape[0]
    own_rows = lax.all_gather(radiosity, "stop", axis=1, tiled=True)
    visited = [own_rows]
    current = own_rows
    for step in range(reach):
        current = shifted(current, "row", -1)
        visited.append(current)
    stacked = jnp.concatenate(visited, axis=0)
    window = lax.dynamic_slice_in_dim(stacked, stop_index, per_row, 0)
    opposite = stacked[reach * per_row : (reach + 1) * per_row]
    blocks = pair_blocks[:, 0]
    forward = jnp.einsum("qij,qjc->qic", blocks, window, preferred_element_type=jnp.float32)
    mirrored = jnp.einsum("qji,qjc->qic", blocks, own_rows, preferred_element_type=jnp.float32)
    far_term = jnp.einsum("qij,qjc->qic", far_blocks, opposite, preferred_element_type=jnp.float32)
    holder = jnp.zeros(((reach + 1) * per_row,) + mirrored.shape[1:], jnp.float32)
    holder = lax.dynamic_update_slice_in_dim(holder, mirrored, stop_index, 0)
    carried = holder[reach * per_row :]
    for step in range(reach - 1, -1, -1):
        carried = shifted(carried, "row", 1) + holder[step * per_row : (step + 1) * per_row]
    owner_total = lax.psum_scatter(carried + forward, "stop", scatter_dimension=1, tiled=True)
    irradiation = (owner_total + far_term) / areas[..., None]
    kinds = reflect_table.shape[0]
    onehot = (patch_material[..., None] == jnp.arange(kinds, dtype=jnp.int32)).astype(jnp.float32)
    reflect = jnp.einsum("qim,mn->qin", onehot, reflect_table, precision=lax.Precision.HIGHEST)
    repeats = emission.shape[2] // reflect_table.shape[1]
    reflect = jnp.tile(reflect, (1, 1, repeats))
    return emission.astype(jnp.float32) + reflect * irradiation


def solution(mesh):
    return jax.shard_map(
        on_device,
        mesh=mesh,
        in_specs=(
            P("row", "stop", None),
            P("row", "stop", None),
            P("row", "stop"),
            P("row", "stop"),
            P(),
            P("row", "stop", None, None),
            P("row", "stop", None),
        ),
        out_specs=P("row", "stop", None),
        check_vma=False,
    )
```

profile of v0, /device:TPU:1, one launch (start us, length us, event | category | flops | bytes accessed | tf_op | source)
XLA Modules:
  0.0 632.9 jit_solution(12865346627203906090)
XLA Ops:
  6.5 0.0 copy-start
  6.5 0.7 all-gather.2.cloned.1.call-update
  7.3 0.0 all-reduce.3.cloned.1.call-start
  7.3 54.5 %all-gather.2.cloned.1.call-done = bf16[4,1024,256]{2,1,0:T(8,128)(2,1)} async-done(((bf16[4,64,256]{2,1,0:T(8,128)(2,1)}), bf16[4,1024,256]{2,1,0:T(8,128)(2,1)}) %all-gather.2.cloned.1.call-update) | async-done | bytes 2097168 | tf_op jit(solution)/shard_map/all_gather | solution.py:16
  61.9 9.9 %broadcast_in_dim.2 = f32[20,1024,256]{1,2,0:T(8,128)} broadcast(f32[]{:T(128)} %constant.4.clone.1), dimensions={} | broadcast | bytes 20971524 | tf_op jit(solution)/shard_map/broadcast_in_dim | solution.py:29
  71.8 4.4 fusion.5
  76.2 2.5 slice.20
  78.7 1.3 collective-permute-start
  80.1 92.8 %collective-permute-done = f32[4,1024,256]{1,2,0:T(8,128)S(1)} collective-permute-done((f32[4,1024,256]{1,2,0:T(8,128)S(1)}, f32[4,1024,256]{1,2,0:T(8,128)S(1)}, u32[]{:S(2)}, u32[]{:S(2)}) %collective-permute-start) | collective-permute-done | bytes 4194336 | tf_op jit(solution)/shard_map/ppermute | solution.py:9
  172.9 3.1 slice_add_fusion.3
  176.0 0.1 collective-permute-start.1
  176.1 3.6 collective-permute-start.4
  179.7 89.6 %collective-permute-done.1 = f32[4,1024,256]{1,2,0:T(8,128)S(1)} collective-permute-done((f32[4,1024,256]{1,2,0:T(8,128)S(1)}, f32[4,1024,256]{1,2,0:T(8,128)S(1)}, u32[]{:S(2)}, u32[]{:S(2)}) %collective-permute-start.1) | collective-permute-done | bytes 4194336 | tf_op jit(solution)/shard_map/ppermute | solution.py:9
  269.3 3.1 slice_add_fusion.2
  272.4 0.1 collective-permute-start.2
  272.5 0.0 collective-permute-done.4
  272.5 3.6 collective-permute-start.5
  276.1 42.8 %collective-permute-done.5 = bf16[4,1024,256]{2,1,0:T(8,128)(2,1)S(1)} collective-permute-done((bf16[4,1024,256]{2,1,0:T(8,128)(2,1)S(1)}, bf16[4,1024,256]{2,1,0:T(8,128)(2,1)S(1)}, u32[]{:S(2)}, u32[]{:S(2)}) %collective-permute-start.5) | collective-permute-done | bytes 2097184 | tf_op jit(solution)/shard_map/ppermute | solution.py:9
  318.8 4.3 collective-permute-start.6
  323.1 41.6 %collective-permute-done.2 = f32[4,1024,256]{1,2,0:T(8,128)S(1)} collective-permute-done((f32[4,1024,256]{1,2,0:T(8,128)S(1)}, f32[4,1024,256]{1,2,0:T(8,128)S(1)}, u32[]{:S(2)}, u32[]{:S(2)}) %collective-permute-start.2) | collective-permute-done | bytes 4194336 | tf_op jit(solution)/shard_map/ppermute | solution.py:9
  364.8 3.1 slice_add_fusion.1
  367.9 0.1 collective-permute-start.3
  368.0 0.0 collective-permute-done.6
  368.0 3.6 collective-permute-start.7
  371.5 0.1 constant_dynamic-update-slice_fusion.4
  371.7 0.1 constant_dynamic-update-slice_fusion.3
  371.8 0.1 constant_dynamic-update-slice_fusion.2
  372.0 0.1 constant_dynamic-update-slice_fusion.1
  372.1 41.3 %collective-permute-done.7 = bf16[4,1024,256]{2,1,0:T(8,128)(2,1)S(1)} collective-permute-done((bf16[4,1024,256]{2,1,0:T(8,128)(2,1)S(1)}, bf16[4,1024,256]{2,1,0:T(8,128)(2,1)S(1)}, u32[]{:S(2)}, u32[]{:S(2)}) %collective-permute-start.7) | collective-permute-done | bytes 2097184 | tf_op jit(solution)/shard_map/ppermute | solution.py:9
  413.4 1.4 copy-done.2
  414.7 0.1 constant_dynamic-update-slice_fusion
  414.9 4.0 copy-done.5
  418.8 40.6 %collective-permute-done.3 = f32[4,1024,256]{1,2,0:T(8,128)} collective-permute-done((f32[4,1024,256]{1,2,0:T(8,128)S(1)}, f32[4,1024,256]{1,2,0:T(8,128)}, u32[]{:S(2)}, u32[]{:S(2)}) %collective-permute-start.3) | collective-permute-done | bytes 4194336 | tf_op jit(solution)/shard_map/ppermute | solution.py:9
  459.4 9.3 %fusion.4 = f32[4,1024,256]{1,2,0:T(8,128)} fusion(f32[4,1024,256]{1,2,0:T(8,128)} %collective-permute-done.3, f32[20,1024,256]{1,2,0:T(8,128)} %fusion.5, bf16[4,1,1024,1024]{3,2,1,0:T(8,128)(2,1)S(1)} %copy-done.1, bf16[20,1024,256]{2,1,0:T(8,128)(2,1)} %copy-done.5, s32[]{:T(128)S(6)} %select_n.4), kind=kOutput, calls=%fused_computation.5 | convolution fusion | flops 2149580800 | bytes 23068676 | tf_op jit(solution)/shard_map/qij,qjc->qic/dot_general | solution.py:26
  468.7 5.2 copy.23
  474.0 0.0 copy-start.6
  474.0 0.0 copy-start.8
  474.0 0.0 all-reduce.3.cloned.1.call-update
  474.0 0.6 copy-done.7
  474.6 0.0 copy-done.9
  474.6 0.2 fusion.14
  474.9 0.1 tile.4
  474.9 0.2 copy.25
  475.1 0.0 copy-done.10
  475.1 0.6 dynamic-slice
  476.4 147.5 %all-reduce.3.cloned.1.call-done = f32[4,1024,256]{2,0,1:T(4,128)} async-done(((f32[4,1024,256]{2,0,1:T(4,128)}), f32[4,1024,256]{2,0,1:T(4,128)}) %all-reduce.3.cloned.1.call-update) | async-done | bytes 4194320
  623.9 1.0 constant_dynamic-slice_fusion
  624.9 1.2 fusion.13
  (15 shorter events, 0.0 us)
Async XLA Ops:
  6.5 618.3 %copy-start = (bf16[4,64,1024]{2,1,0:T(8,128)(2,1)S(1)}, bf16[4,64,1024]{2,1,0:T(8,128)(2,1)}, u32[]{:S(2)}) copy-start(bf16[4,64,1024]{2,1,0:T(8,128)(2,1)} %param.13) | copy-start | bytes 1572868
  6.5 55.3 %all-gather.2.cloned.1.call-start = ((), (), s32[]{:S(2)}) async-start(), calls=%async_computation | async-start | bytes 2228224 | tf_op jit(solution)/shard_map/all_gather | solution.py:16
  7.3 616.6 %all-reduce.3.cloned.1.call-start = ((), (), s32[]{:S(2)}) async-start(), calls=%async_computation.1 | async-start | bytes 8388608
  61.8 9.9 %copy-start.1 = (bf16[4,1,1024,1024]{3,2,1,0:T(8,128)(2,1)S(1)}, bf16[4,1,1024,1024]{3,2,1,0:T(8,128)(2,1)}, u32[]{:S(2)}) copy-start(bf16[4,1,1024,1024]{3,2,1,0:T(8,128)(2,1)} %param.12) | copy-start | bytes 25165828
  61.8 9.9 %copy-start.4 = (bf16[4,1024,256]{2,1,0:T(8,128)(2,1)S(1)}, bf16[4,1024,256]{2,1,0:T(8,128)(2,1)}, u32[]{:S(2)}) copy-start(bf16[4,1024,256]{2,1,0:T(8,128)(2,1)} %all-gather.2.cloned.1.call-done) | copy-start | bytes 6291460
  78.7 94.2 %collective-permute-start = (f32[4,1024,256]{1,2,0:T(8,128)S(1)}, f32[4,1024,256]{1,2,0:T(8,128)S(1)}, u32[]{:S(2)}, u32[]{:S(2)}) collective-permute-start(f32[4,1024,256]{1,2,0:T(8,128)S(1)} %slice.20), channel_id=1, source_target_pairs={{0,16},{16,32},{32,48},{48,64},{64,80},{80,96},{96,112},{112,0},{1... | collective-permute-start | bytes 12582920 | tf_op jit(solution)/shard_map/ppermute | solution.py:9
  176.0 93.3 %collective-permute-start.1 = (f32[4,1024,256]{1,2,0:T(8,128)S(1)}, f32[4,1024,256]{1,2,0:T(8,128)S(1)}, u32[]{:S(2)}, u32[]{:S(2)}) collective-permute-start(f32[4,1024,256]{1,2,0:T(8,128)S(1)} %slice_add_fusion.3), channel_id=1, source_target_pairs={{0,16},{16,32},{32,48},{48,64},{64,80},{80,96},{96,112},{112,0},{1... | collective-permute-start | bytes 12582920 | tf_op jit(solution)/shard_map/ppermute | solution.py:9
  176.1 96.4 %collective-permute-start.4 = (bf16[4,1024,256]{2,1,0:T(8,128)(2,1)S(1)}, bf16[4,1024,256]{2,1,0:T(8,128)(2,1)S(1)}, u32[]{:S(2)}, u32[]{:S(2)}) collective-permute-start(bf16[4,1024,256]{2,1,0:T(8,128)(2,1)S(1)} %copy-done.4), channel_id=1, source_target_pairs={{0,112},{16,0},{32,16},{48,32},{64,48},{80,64},{96,80},{112,96},{1... | collective-permute-start | bytes 6291464 | tf_op jit(solution)/shard_map/ppermute | solution.py:9
  272.4 92.4 %collective-permute-start.2 = (f32[4,1024,256]{1,2,0:T(8,128)S(1)}, f32[4,1024,256]{1,2,0:T(8,128)S(1)}, u32[]{:S(2)}, u32[]{:S(2)}) collective-permute-start(f32[4,1024,256]{1,2,0:T(8,128)S(1)} %slice_add_fusion.2), channel_id=1, source_target_pairs={{0,16},{16,32},{32,48},{48,64},{64,80},{80,96},{96,112},{112,0},{1... | collective-permute-start | bytes 12582920 | tf_op jit(solution)/shard_map/ppermute | solution.py:9
  272.5 46.3 %collective-permute-start.5 = (bf16[4,1024,256]{2,1,0:T(8,128)(2,1)S(1)}, bf16[4,1024,256]{2,1,0:T(8,128)(2,1)S(1)}, u32[]{:S(2)}, u32[]{:S(2)}) collective-permute-start(bf16[4,1024,256]{2,1,0:T(8,128)(2,1)S(1)} %collective-permute-done.4), channel_id=1, source_target_pairs={{0,112},{16,0},{32,16},{48,32},{64,48},{80,64},{96,80},{112,96},{1... | collective-permute-start | bytes 6291464 | tf_op jit(solution)/shard_map/ppermute | solution.py:9
  318.8 49.2 %collective-permute-start.6 = (bf16[4,1024,256]{2,1,0:T(8,128)(2,1)S(1)}, bf16[4,1024,256]{2,1,0:T(8,128)(2,1)S(1)}, u32[]{:S(2)}, u32[]{:S(2)}) collective-permute-start(bf16[4,1024,256]{2,1,0:T(8,128)(2,1)S(1)} %collective-permute-done.5), channel_id=1, source_target_pairs={{0,112},{16,0},{32,16},{48,32},{64,48},{80,64},{96,80},{112,96},{1... | collective-permute-start | bytes 6291464 | tf_op jit(solution)/shard_map/ppermute | solution.py:9
  367.9 91.5 %collective-permute-start.3 = (f32[4,1024,256]{1,2,0:T(8,128)S(1)}, f32[4,1024,256]{1,2,0:T(8,128)}, u32[]{:S(2)}, u32[]{:S(2)}) collective-permute-start(f32[4,1024,256]{1,2,0:T(8,128)S(1)} %slice_add_fusion.1), channel_id=1, source_target_pairs={{0,16},{16,32},{32,48},{48,64},{64,80},{80,96},{96,112},{112,0},{1... | collective-permute-start | bytes 12582920 | tf_op jit(solution)/shard_map/ppermute | solution.py:9
  368.0 45.4 %collective-permute-start.7 = (bf16[4,1024,256]{2,1,0:T(8,128)(2,1)S(1)}, bf16[4,1024,256]{2,1,0:T(8,128)(2,1)S(1)}, u32[]{:S(2)}, u32[]{:S(2)}) collective-permute-start(bf16[4,1024,256]{2,1,0:T(8,128)(2,1)S(1)} %collective-permute-done.6), channel_id=1, source_target_pairs={{0,112},{16,0},{32,16},{48,32},{64,48},{80,64},{96,80},{112,96},{1... | collective-permute-start | bytes 6291464 | tf_op jit(solution)/shard_map/ppermute | solution.py:9
  413.4 1.4 copy-start.2
  414.9 4.0 copy-start.5
  473.9 0.7 copy-start.7
  473.9 0.7 copy-start.9
  474.0 1.2 copy-start.10
  474.0 150.9 %copy-start.3 = (bf16[4,1024,256]{2,1,0:T(8,128)(2,1)S(1)}, bf16[4,1024,256]{2,1,0:T(8,128)(2,1)}, u32[]{:S(2)}) copy-start(bf16[4,1024,256]{2,1,0:T(8,128)(2,1)} %copy-done.2) | copy-start | bytes 6291460
  474.0 150.9 %copy-start.6 = (bf16[4,64,256]{2,1,0:T(8,128)(2,1)S(1)}, bf16[4,64,256]{2,1,0:T(8,128)(2,1)}, u32[]{:S(2)}) copy-start(bf16[4,64,256]{2,1,0:T(8,128)(2,1)} %param.8) | copy-start | bytes 393220
  474.0 150.9 %copy-start.8 = (f32[4,64]{1,0:T(4,128)S(1)}, f32[4,64]{1,0:T(4,128)}, u32[]{:S(2)}) copy-start(f32[4,64]{1,0:T(4,128)} %param.9) | copy-start | bytes 3076
Sparse Core Ops, SparseCore 0:
  9.8 51.9 all-gather.1
  474.1 149.6 all-reduce.2
where the time goes:
time: 633 us
  waiting for transfers between devices  551 us (87%)
  local copies, waits for them, and re-layouts  26.1 us (4%)
  starting transfers between devices  16.6 us (3%)
  matrix products  15.1 us (2%)
  between operations  14.3 us (2%)
  other arithmetic  9.35 us (1%)
    ppermute x8, waiting for transfers between devices, shifted(): lax.ppermute(shard, axis, [(i, (i + by) % peers) for i in range(peers)])  349 us
    unnamed x3, waiting for transfers between devices  148 us
    all_gather x1, waiting for transfers between devices, on_device(): own_rows = lax.all_gather(radiosity, 'stop', axis=1, tiled=True)  54.5 us
    ppermute x8, starting transfers between devices, shifted(): lax.ppermute(shard, axis, [(i, (i + by) % peers) for i in range(peers)])  16.6 us
  transfers between devices with their start and end apart: 10, of which 8 were waited for; matrix products, arithmetic and copies ran while one was open for 1% of the time, Pallas kernels for 0%

commit v1 on v0

v1 whole, which is shorter than its diff:
```python
import functools

import jax
import jax.numpy as jnp
from jax import lax
from jax.experimental import pallas as pl
from jax.experimental.pallas import tpu as pltpu
from jax.sharding import PartitionSpec as P

MESH = pl.DeviceIdType.MESH
F32 = jnp.float32


class Links:
    def __init__(self, send_sem, recv_sem):
        self.send_sem, self.recv_sem = send_sem, recv_sem
        self.names, self.recv_count, self.sent = {}, 0, []

    def name(self, key, count=1):
        self.names[key] = self.recv_count
        self.recv_count += count

    def copy(self, key, src, dst, target, extra=0):
        made = pltpu.make_async_remote_copy(
            src_ref=src,
            dst_ref=dst,
            send_sem=self.send_sem.at[len(self.sent)],
            recv_sem=self.recv_sem.at[self.names[key] + extra],
            device_id=target,
            device_id_type=MESH,
        )
        self.sent.append(made)
        return made

    def send(self, key, src, dst, target, extra=0):
        self.copy(key, src, dst, target, extra).start()

    def arrived(self, key, dst, target, extra=0):
        pltpu.make_async_remote_copy(
            src_ref=dst,
            dst_ref=dst,
            send_sem=self.send_sem.at[0],
            recv_sem=self.recv_sem.at[self.names[key] + extra],
            device_id=target,
            device_id_type=MESH,
        ).wait_recv()


def kernel(
    rows, columns,
    rad, emi, area, mat, tab, pair, far, out,
    blocks, own, win, grp, fbuf, rf, fw, fs, fy, fx, mr, ms, un, mx, hz_own, hz, emi_v,
    send_sem, recv_sem, local_sem,
):
    nq, slice_rows, width = rad.shape
    patches = pair.shape[2]
    half_patches = patches // 2
    slots = nq + 1
    groups = 2 * columns + nq - 1
    parts = [(g * nq, min(nq, groups - g * nq)) for g in range(-(-groups // nq))]
    row, stop = lax.axis_index("row"), lax.axis_index("stop")
    half, col, core = stop // (2 * columns), (stop // 2) % columns, stop % 2
    others = range(1, columns)

    def at(row_by, half_to, col_to, core_to):
        return (row_by, half_to * (2 * columns) + col_to * 2 + core_to)

    def row_up(by):
        return lax.rem(row + by, rows)

    def row_down(by):
        return lax.rem(row + rows - by, rows)

    def col_up(by):
        return lax.rem(col + by, columns)

    def col_down(by):
        return lax.rem(col + columns - by, columns)

    sibling = at(row, half, col, 1 - core)
    partner = at(row, 1 - half, col, core)
    me_col = {by: at(row, half, col_up(by), core) for by in others}

    links = Links(send_sem, recv_sem)
    for by in others:
        for key in ("own_x", "rf_x", "win_x"):
            links.name((key, by))
        for i in range(slots):
            links.name(("mx", by, i))
        for q in range(nq):
            links.name(("fx", by, q))
    for by in range(columns):
        for key in ("own_y", "own_sx", "own_sy", "rf_s", "win_s"):
            links.name((key, by))
    links.name("rf")
    links.name("far_y")
    for g in range(len(parts)):
        links.name(("grp", g), 2)
        links.name(("hz", g), 2)
    for q in range(nq):
        for key in ("ms", "fs", "fy"):
            links.name((key, q))

    local_count = [0]

    def local(src, dst):
        made = pltpu.make_async_copy(src, dst, local_sem.at[local_count[0]])
        local_count[0] += 1
        return made

    own_copy = local(rad, own.at[:, half, col, core])
    own_copy.start()
    rows_of_far = pl.ds(pl.multiple_of(half * half_patches, half_patches), half_patches)
    rows_of_other = pl.ds(pl.multiple_of((1 - half) * half_patches, half_patches), half_patches)
    block_copies = []
    for q in range(nq):
        made = local(pair.at[q, 0], blocks.at[q])
        made.start()
        block_copies.append(made)
    far_copy = local(far.at[:, :, rows_of_far], fbuf.at[half])
    far_copy.start()
    emi_copy = local(emi, emi_v)
    emi_copy.start()

    barrier = pltpu.get_barrier_semaphore()
    peers = [sibling] + [me_col[by] for by in others]
    for by in range(rows):
        for flip in range(2):
            if by or flip:
                peers.append(at(row_up(by), half if flip == 0 else 1 - half, col, core))
    for peer in peers:
        pl.semaphore_signal(barrier, inc=1, device_id=peer, device_id_type=MESH)
    pl.semaphore_wait(barrier, len(peers))

    for by in others:
        links.send(("own_x", by), rad, own.at[:, half, col, core], me_col[by])
    links.send(("own_y", 0), rad, own.at[:, half, col, core], partner)
    links.send("rf", rad, rf.at[:, col, core], at(row_down(rows // 2), half, col, core))
    self_grp = None
    for half_to in range(2):
        for g, (first, count) in enumerate(parts):
            by = half_to * (2 * columns) // nq + g
            src = rad.at[pl.ds(0, count)]
            dst = grp.at[pl.ds(first, count), half]
            remote = links.copy(("grp", g), src, dst, at(row_down(by), half_to, col, core), half)
            if by == 0:
                self_grp = (remote, local(src, dst))

                @pl.when(half == 1)
                def _(remote=remote):
                    remote.start()

                @pl.when(half == 0)
                def _(near=self_grp[1]):
                    near.start()
            else:
                remote.start()
    links.send("far_y", far.at[:, :, rows_of_other], fbuf.at[half], partner)
    links.send(("own_sx", 0), rad, own.at[:, half, col, core], sibling)

    for by in others:
        src_col = col_down(by)
        piece = own.at[:, half, src_col, core]
        links.arrived(("own_x", by), piece, me_col[by])
        links.send(("own_y", by), piece, piece, partner)
        links.send(("own_sx", by), piece, piece, sibling)

    piece = rf.at[:, col, core]
    links.arrived("rf", piece, sibling)
    for by in others:
        links.send(("rf_x", by), piece, piece, me_col[by])
    links.send(("rf_s", 0), piece, piece, sibling)

    for half_from in range(2):
        for g, (first, count) in enumerate(parts):
            piece = grp.at[pl.ds(first, count), half_from]
            if g == 0 and half_from == 0:

                @pl.when(half == 1)
                def _(piece=piece):
                    links.arrived(("grp", 0), piece, sibling, 0)

                @pl.when(half == 0)
                def _():
                    self_grp[1].wait()
            else:
                links.arrived(("grp", g), piece, sibling, half_from)
    for by in others:
        links.send(
            ("win_x", by),
            grp.at[pl.ds(2 * col_up(by), slots)],
            win.at[:, :, col, core],
            me_col[by],
        )
    win_copy = local(grp.at[pl.ds(2 * col, slots)], win.at[:, :, col, core])
    win_copy.start()
    links.send(
        ("win_s", 0),
        grp.at[pl.ds(2 * col + 1 - core, nq)],
        win.at[pl.ds(1 - core, nq), :, col, core],
        sibling,
    )

    for by in range(columns):
        src_col = col_down(by)
        piece = own.at[:, 1 - half, src_col, core]
        links.arrived(("own_y", by), piece, partner)
        links.send(("own_sy", by), piece, piece, sibling)

    own_copy.wait()
    for by in range(columns):
        src_col = col_down(by)
        links.arrived(("own_sx", by), own.at[:, half, src_col, 1 - core], sibling)
        links.arrived(("own_sy", by), own.at[:, 1 - half, src_col, 1 - core], sibling)

    per_tile = columns // 2
    tile = per_tile * 2 * slice_rows
    tiles = patches // tile

    def tile_at(n):
        return pl.ds(pl.multiple_of(n * tile, tile), tile)

    for q in range(nq):
        block_copies[q].wait()

        def mirrored(n, carry, q=q):
            product = lax.dot_general(
                blocks[q, :, tile_at(n)],
                own[q].reshape(patches, width),
                (((0,), (0,)), ((), ())),
                preferred_element_type=F32,
            )
            mr[q, n // 2, pl.ds((n % 2) * per_tile, per_tile)] = product.reshape(
                per_tile, 2, slice_rows, width
            )
            return carry

        lax.fori_loop(0, tiles, mirrored, 0)
        links.send(("ms", q), mr.at[q, :, :, 1 - core], ms.at[q], sibling)

    for i in range(slots):
        if i < nq:
            links.arrived(("ms", i), ms.at[i], sibling)
        if i == 0:

            @pl.when(core == 0)
            def _():
                un[0] = mr[0, :, :, 0]

            @pl.when(core == 1)
            def _():
                un[0] = ms[0]
        elif i == nq:

            @pl.when(core == 0)
            def _():
                un[nq] = ms[nq - 1]

            @pl.when(core == 1)
            def _():
                un[nq] = mr[nq - 1, :, :, 1]
        else:
            un[i] = mr[i - core, :, :, core] + ms[i - 1 + core]
        for by in others:
            links.send(
                ("mx", by, i), un.at[i, :, col_up(by)], mx.at[by - 1, i], me_col[by]
            )

    for by in others:
        piece = rf.at[:, col_down(by), core]
        links.arrived(("rf_x", by), piece, sibling)
        links.send(("rf_s", by), piece, piece, sibling)
    for by in others:
        src_col = col_down(by)
        links.arrived(("win_x", by), win.at[:, :, src_col, core], sibling)
        piece = win.at[pl.ds(1 - core, nq), :, src_col, core]
        links.send(("win_s", by), piece, piece, sibling)

    win_copy.wait()
    for by in range(columns):
        src_col = col_down(by)
        links.arrived(
            ("win_s", by), win.at[pl.ds(core, nq), :, src_col, 1 - core], sibling
        )
    for q in range(nq):

        def forward(n, carry, q=q):
            product = jnp.dot(
                blocks[q, tile_at(n), :],
                win[core + q].reshape(patches, width),
                preferred_element_type=F32,
            )
            fw[q, n // 2, pl.ds((n % 2) * per_tile, per_tile)] = product.reshape(
                per_tile, 2, slice_rows, width
            )
            return carry

        lax.fori_loop(0, tiles, forward, 0)
        links.send(("fs", q), fw.at[q, :, :, 1 - core], fs.at[q], sibling)

    for by in range(columns):
        links.arrived(("rf_s", by), rf.at[:, col_down(by), 1 - core], sibling)
    far_copy.wait()
    links.arrived("far_y", fbuf.at[1 - half], partner)
    for q in range(nq):
        links.arrived(("fs", q), fs.at[q], sibling)
        fw[q, :, :, core] = fw[q, :, :, core] + fs[q]
        opposite = jnp.dot(
            fbuf[:, q].reshape(2 * slice_rows, half_patches),
            rf[q].reshape(half_patches, width),
            preferred_element_type=F32,
        )
        fw[q, :, col, core] = fw[q, :, col, core] + opposite.reshape(2, slice_rows, width)
        links.send(("fy", q), fw.at[q, 1 - half, :, core], fy.at[q], partner)

    for q in range(nq):
        links.arrived(("fy", q), fy.at[q], partner)
        fw[q, half, :, core] = fw[q, half, :, core] + fy[q]
        for by in others:
            links.send(
                ("fx", by, q), fw.at[q, half, col_up(by), core], fx.at[by - 1, q], me_col[by]
            )

    hz_own[...] = jnp.zeros_like(hz_own)
    hz_own[pl.ds(2 * col, slots)] = un[:, :, col]
    for by in others:
        src_col = col_down(by)
        for i in range(slots):
            links.arrived(("mx", by, i), mx.at[by - 1, i], sibling)
        reach = pl.ds(2 * src_col, slots)
        hz_own[reach] = hz_own[reach] + mx[by - 1]
    self_hz = None
    first_row = half * (2 * columns) // nq
    for half_to in range(2):
        for g, (first, count) in enumerate(parts):
            src = hz_own.at[pl.ds(first, count), half_to]
            dst = hz.at[half, pl.ds(first, count)]
            target = at(row_up(first_row + g), half_to, col, core)
            remote = links.copy(("hz", g), src, dst, target, half)
            if g == 0 and half_to == 0:
                self_hz = (remote, local(src, dst))

                @pl.when(half == 1)
                def _(remote=remote):
                    remote.start()

                @pl.when(half == 0)
                def _(near=self_hz[1]):
                    near.start()
            else:
                remote.start()

    emi_copy.wait()
    for by in others:
        for q in range(nq):
            links.arrived(("fx", by, q), fx.at[by - 1, q], sibling)
    for half_from in range(2):
        for g, (first, count) in enumerate(parts):
            piece = hz.at[half_from, pl.ds(first, count)]
            if g == 0 and half_from == 0:

                @pl.when(half == 1)
                def _(piece=piece):
                    links.arrived(("hz", 0), piece, sibling, 0)

                @pl.when(half == 0)
                def _():
                    self_hz[1].wait()
            else:
                links.arrived(("hz", g), piece, sibling, half_from)

    kinds, bands = tab.shape
    reflect_of = jnp.concatenate([tab[...]] * (width // bands), axis=1)
    across = lax.broadcasted_iota(jnp.int32, (slice_rows, slice_rows), 1)
    down = lax.broadcasted_iota(jnp.int32, (slice_rows, slice_rows), 0)

    def upright(values):
        spread = jnp.broadcast_to(values, (slice_rows, slice_rows))
        return jnp.sum(jnp.where(across == down, spread, 0), axis=1, keepdims=True)

    for q in range(nq):
        total = fw[q, half, col, core]
        for by in others:
            total = total + fx[by - 1, q]
        for half_from in range(2):
            for u in range(q, groups, nq):
                total = total + hz[half_from, u]
        kind = upright(mat[pl.ds(q, 1), :])
        reflect = jnp.zeros((slice_rows, width), F32)
        for m in range(kinds):
            reflect = jnp.where(kind == m, reflect_of[m : m + 1, :], reflect)
        irradiation = total / upright(area[pl.ds(q, 1), :])
        out[q] = emi_v[q].astype(F32) + reflect * irradiation

    conditional = (self_grp[0], self_hz[0])
    for made in links.sent:
        if made is conditional[0] or made is conditional[1]:

            @pl.when(half == 1)
            def _(made=made):
                made.wait_send()
        else:
            made.wait_send()


def on_device(rows, columns, radiosity, emission, areas, patch_material, reflect_table, pair_blocks, far_blocks):
    nq, slice_rows, width = radiosity.shape
    patches = pair_blocks.shape[2]
    slots = nq + 1
    groups = 2 * columns + nq - 1
    half_patches = patches // 2
    bf16 = jnp.bfloat16
    scratch = [
        pltpu.VMEM((nq, patches, patches), bf16),
        pltpu.VMEM((nq, 2, columns, 2, slice_rows, width), bf16),
        pltpu.VMEM((slots, 2, columns, 2, slice_rows, width), bf16),
        pltpu.VMEM((groups, 2, slice_rows, width), bf16),
        pltpu.VMEM((2, nq, slice_rows, half_patches), bf16),
        pltpu.VMEM((nq, columns, 2, slice_rows, width), bf16),
        pltpu.VMEM((nq, 2, columns, 2, slice_rows, width), F32),
        pltpu.VMEM((nq, 2, columns, slice_rows, width), F32),
        pltpu.VMEM((nq, columns, slice_rows, width), F32),
        pltpu.VMEM((columns - 1, nq, slice_rows, width), F32),
        pltpu.VMEM((nq, 2, columns, 2, slice_rows, width), F32),
        pltpu.VMEM((nq, 2, columns, slice_rows, width), F32),
        pltpu.VMEM((slots, 2, columns, slice_rows, width), F32),
        pltpu.VMEM((columns - 1, slots, 2, slice_rows, width), F32),
        pltpu.VMEM((groups, 2, slice_rows, width), F32),
        pltpu.VMEM((2, groups, slice_rows, width), F32),
        pltpu.VMEM((nq, slice_rows, width), bf16),
        pltpu.SemaphoreType.DMA((160,)),
        pltpu.SemaphoreType.DMA((160,)),
        pltpu.SemaphoreType.DMA((16,)),
    ]
    any_space = pl.BlockSpec(memory_space=pl.ANY)
    vmem = pl.BlockSpec(memory_space=pltpu.VMEM)
    flops = 4 * nq * patches * patches * width
    return pl.pallas_call(
        functools.partial(kernel, rows, columns),
        out_shape=jax.ShapeDtypeStruct((nq, slice_rows, width), F32),
        in_specs=[any_space, any_space, vmem, vmem, vmem, any_space, any_space],
        out_specs=vmem,
        scratch_shapes=scratch,
        compiler_params=pltpu.CompilerParams(
            collective_id=0, has_side_effects=True, vmem_limit_bytes=58 * 2**20
        ),
        cost_estimate=pl.CostEstimate(
            flops=flops, bytes_accessed=2 * nq * patches * patches, transcendentals=0
        ),
    )(radiosity, emission, areas, patch_material, reflect_table, pair_blocks, far_blocks)


def solution(mesh):
    rows, stops = mesh.shape["row"], mesh.shape["stop"]
    return jax.shard_map(
        functools.partial(on_device, rows, stops // 4),
        mesh=mesh,
        in_specs=(
            P("row", "stop", None),
            P("row", "stop", None),
            P("row", "stop"),
            P("row", "stop"),
            P(),
            P("row", "stop", None, None),
            P("row", "stop", None),
        ),
        out_specs=P("row", "stop", None),
        check_vma=False,
    )
```

time: 633 us -> 110 us (0.17)
  the two profiles are of different devices: /device:TPU:1 before, /device:TPU:17 now
where the time goes in v1:
time: 110 us
  Pallas kernels  108 us (98%)
  local copies, waits for them, and re-layouts  1.67 us (2%)
    pallas_call x1, Pallas kernels, on_device(): pl.pallas_call(functools.partial(kernel, rows, columns), out_shape=jax.Sh...  108 us

profile of v1, /device:TPU:17, one launch (start us, length us, event | category | flops | bytes accessed | tf_op | source)
XLA Modules:
  0.0 110.0 jit_solution(7215868696578497841)
XLA Ops:
  0.0 108.4 %shard_map.73 = f32[4,64,256]{2,1,0:T(8,128)} custom-call(bf16[4,64,256]{2,1,0:T(8,128)(2,1)} %rad.1, bf16[4,64,256]{2,1,0:T(8,128)(2,1)} %emi.1, f32[4,64]{1,0:T(4,128)} %area.1, s32[4,64]{1,0:T(4,128)} %mat.1, f32[16,32]{1,0:T(8,128)} %tab.1, bf16[4,1,1024,1024]{3,2,1,0:T(8,128)(2,1)} %pair.1, bf16[4,64,1024]{2,1,0:T(8,128)(2,1)} %far.1), custom_call_target="tpu_custom_call" | custom-call | flops 4294967296 | bytes 8388608 | tf_op jit(solution)/shard_map/pallas_call | solution.py:438
  108.4 1.7 %copy.9 = f32[4,64,256]{2,1,0:T(8,128)} copy(f32[4,64,256]{2,1,0:T(8,128)} %shard_map.73) | data formatting | bytes 524288

commit v2 on v0

v2 whole, which is shorter than its diff:
```python
import functools

import jax
import jax.numpy as jnp
from jax import lax
from jax.experimental import pallas as pl
from jax.experimental.pallas import tpu as pltpu
from jax.sharding import PartitionSpec as P

MESH = pl.DeviceIdType.MESH
F32 = jnp.float32


SPLIT = 0
XFIRST = ()
QORDER = (0, 1, 2, 3)
ORDER = (
    "own_send",
    "reach_send 0",
    "reach_send 1",
    "own_pass_y",
    "own_pass_x",
    "reach_pass 0",
    "own_end",
    "reach_pass 1",
    "opposite_send",
    "mirror",
    "unite",
    "opposite_pass",
    "window_pass",
    "sums_send 0",
    "sums_send 1",
    "far_send",
    "sums_send 2",
    "sums_send 3",
    "forward",
    "forward_unite 0",
    "forward_unite 1",
    "forward_unite 2",
    "forward_unite 3",
    "opposite 0",
    "opposite 1",
    "opposite 2",
    "opposite 3",
    "sums_pass 0",
    "forward_pass 0",
    "sums_pass 1",
    "forward_pass 1",
    "sums_pass 2",
    "forward_pass 2",
    "sums_pass 3",
    "forward_pass 3",
)


class Links:
    def __init__(self, send_sem, recv_sem):
        self.send_sem, self.recv_sem = send_sem, recv_sem
        self.names, self.recv_count, self.sent = {}, 0, []

    def name(self, key, count=1):
        self.names[key] = self.recv_count
        self.recv_count += count

    def copy(self, key, src, dst, target, extra=0):
        made = pltpu.make_async_remote_copy(
            src_ref=src,
            dst_ref=dst,
            send_sem=self.send_sem.at[len(self.sent)],
            recv_sem=self.recv_sem.at[self.names[key] + extra],
            device_id=target,
            device_id_type=MESH,
        )
        self.sent.append(made)
        return made

    def send(self, key, src, dst, target, extra=0):
        self.copy(key, src, dst, target, extra).start()

    def arrived(self, key, dst, target, extra=0):
        pltpu.make_async_remote_copy(
            src_ref=dst,
            dst_ref=dst,
            send_sem=self.send_sem.at[0],
            recv_sem=self.recv_sem.at[self.names[key] + extra],
            device_id=target,
            device_id_type=MESH,
        ).wait_recv()


def kernel(
    rows, columns,
    rad, emi, area, mat, tab, pair, far, out,
    blocks, own, win, grp, fbuf, rf, fw, fs, fy, fx, mr, ms, un, mx, hz_own, hz, emi_v, refl,
    send_sem, recv_sem, local_sem,
):
    nq, slice_rows, width = rad.shape
    patches = pair.shape[2]
    half_patches = patches // 2
    slots = nq + 1
    groups = 2 * columns + nq - 1
    parts = [(g * nq, min(nq, groups - g * nq)) for g in range(-(-groups // nq))]
    row, stop = lax.axis_index("row"), lax.axis_index("stop")
    half, col, core = stop // (2 * columns), (stop // 2) % columns, stop % 2
    others = range(1, columns)

    def at(row_by, half_to, col_to, core_to):
        return (row_by, half_to * (2 * columns) + col_to * 2 + core_to)

    def row_up(by):
        return lax.rem(row + by, rows)

    def row_down(by):
        return lax.rem(row + rows - by, rows)

    def col_up(by):
        return lax.rem(col + by, columns)

    def col_down(by):
        return lax.rem(col + columns - by, columns)

    sibling = at(row, half, col, 1 - core)
    partner = at(row, 1 - half, col, core)
    me_col = {by: at(row, half, col_up(by), core) for by in others}
    starts = (0, 2 * columns // nq)
    halves = (half, 1 - half)

    def start_of(which):
        return jnp.where(which == 0, starts[0], starts[1])

    split = SPLIT
    links = Links(send_sem, recv_sem)
    for by in others:
        for key in ("own_x", "own_sx", "own_ya", "own_xb", "own_sa", "own_sb"):
            links.name((key, by))
        for flip in range(2):
            links.name(("far", by, flip))
            links.name(("win_x", by, flip))
        for part in range(4):
            links.name(("mx", by, part))
        for q in range(nq):
            links.name(("fx", by, q))
    for by in range(columns):
        links.name(("win_s", by))
    for key in ("own_s", "own_y", "own_sy"):
        links.name((key, 0))
    for key in ("rf", "rf_s"):
        links.name((key, 0), 2)
    for g in range(len(parts)):
        for flip in range(2):
            links.name(("grp", g, flip))
        for part in range(4):
            links.name(("hz", g, part))
    for q in range(nq):
        for key in ("ms", "fs", "fy"):
            links.name((key, q))

    local_count = [0]

    def local(src, dst):
        made = pltpu.make_async_copy(src, dst, local_sem.at[local_count[0]])
        local_count[0] += 1
        return made

    def far_columns(side, column):
        first = side * half_patches + column * (2 * slice_rows)
        return pl.ds(pl.multiple_of(first, 2 * slice_rows), 2 * slice_rows)

    def offsets(mine, theirs):
        reach = {starts[mine] + g for g in range(len(parts))}
        back = {-(starts[theirs] + g) for g in range(len(parts))}
        both = {by % rows for by in reach | back | {rows // 2}}
        return sorted(both - {0} if mine == theirs else both)

    barrier = pltpu.get_barrier_semaphore()
    peers = []
    for a, b in zip(offsets(0, 1), offsets(1, 0), strict=True):
        peers.append(at(row_up(jnp.where(half == 0, a, b)), 1 - half, col, core))
    for a, b in zip(offsets(0, 0), offsets(1, 1), strict=True):
        peers.append(at(row_up(jnp.where(half == 0, a, b)), half, col, core))
    peers += [me_col[by] for by in others] + [sibling]
    for peer in peers:
        pl.semaphore_signal(barrier, inc=1, device_id=peer, device_id_type=MESH)

    own_copy = local(rad, own.at[:, half, col, core])
    own_copy.start()
    block_copies = []
    for q in range(nq):
        made = local(pair.at[q, 0], blocks.at[q])
        made.start()
        block_copies.append(made)
    far_copies = []
    for side in range(2):
        made = local(far.at[:, :, far_columns(side, col)], fbuf.at[side, :, col])
        made.start()
        far_copies.append(made)
    emi_copy = local(emi, emi_v)
    emi_copy.start()
    pl.semaphore_wait(barrier, len(peers))

    mine = own.at[:, half, col, core]
    win_copies, conditional = [], []
    a_part, b_part = pl.ds(0, split), pl.ds(split, nq - split)
    per_tile = columns // 2
    tile = per_tile * 2 * slice_rows
    tiles = patches // tile
    part_rows = slice_rows // 2
    sum_parts = [(flip, pl.ds(n * part_rows, part_rows)) for flip in (1, 0) for n in range(2)]

    def tile_at(n):
        return pl.ds(pl.multiple_of(n * tile, tile), tile)

    def own_send():
        links.send(("own_y", 0), rad, mine, partner)
        for by in others:
            links.send(("own_x", by), rad, mine, me_col[by])
        links.send(("own_s", 0), rad, mine, sibling)

    def reach_send(flip):
        for g, (first, count) in enumerate(parts):
            src = rad.at[pl.ds(0, count)]
            dst = grp.at[pl.ds(first, count), half]
            source_row = row_down(start_of(halves[flip]) + g)
            remote = links.copy(("grp", g, flip), src, dst, at(source_row, halves[flip], col, core))
            if g == 0 and flip == 0:
                near = local(src, dst)
                conditional.append(remote)
                win_copies.append(near)

                @pl.when(half == 1)
                def _(remote=remote):
                    remote.start()

                @pl.when(half == 0)
                def _(near=near):
                    near.start()
            else:
                remote.start()

    def opposite_send():
        for flip in range(2):
            target = at(row_down(rows // 2), halves[flip], col, core)
            links.send(("rf", 0), rad, rf.at[:, half, core], target, half)

    def far_send():
        for by in others:
            for side in range(2):
                src = far.at[:, :, far_columns(side, col_up(by))]
                links.send(("far", by, side), src, fbuf.at[side, :, col], me_col[by])

    def own_pass_y():
        piece = own.at[:, 1 - half, col, core]
        links.arrived(("own_y", 0), piece, partner)
        if split < nq:
            piece_b = own.at[b_part, 1 - half, col, core]
            for by in others:
                links.send(("own_xb", by), piece_b, piece_b, me_col[by])
        links.send(("own_sy", 0), piece, piece, sibling)

    def own_pass_x():
        for by in others:
            piece = own.at[:, half, col_down(by), core]
            links.arrived(("own_x", by), piece, me_col[by])
            if split:
                piece_a = own.at[a_part, half, col_down(by), core]
                links.send(("own_ya", by), piece_a, piece_a, partner)
            links.send(("own_sx", by), piece, piece, sibling)

    def own_end():
        for by in others:
            if split < nq:
                piece = own.at[b_part, 1 - half, col_down(by), core]
                links.arrived(("own_xb", by), piece, me_col[by])
                links.send(("own_sb", by), piece, piece, sibling)
            if split:
                piece = own.at[a_part, 1 - half, col_down(by), core]
                links.arrived(("own_ya", by), piece, partner)
                links.send(("own_sa", by), piece, piece, sibling)

    def reach_pass(flip):
        side = halves[flip]
        for g, (first, count) in enumerate(parts):
            piece = grp.at[pl.ds(first, count), side]
            if g == 0 and flip == 0:

                @pl.when(half == 1)
                def _(piece=piece):
                    links.arrived(("grp", 0, 0), piece, sibling)

                @pl.when(half == 0)
                def _():
                    win_copies[0].wait()
            else:
                links.arrived(("grp", g, flip), piece, sibling)
        for by in others:
            src = grp.at[pl.ds(2 * col_up(by), slots), side]
            links.send(("win_x", by, flip), src, win.at[:, side, col, core], me_col[by])
        made = local(grp.at[pl.ds(2 * col, slots), side], win.at[:, side, col, core])
        made.start()
        win_copies.append(made)
        if flip == 1:
            src = grp.at[pl.ds(2 * col + 1 - core, nq)]
            links.send(("win_s", 0), src, win.at[pl.ds(1 - core, nq), :, col, core], sibling)

    def mirror():
        own_copy.wait()
        links.arrived(("own_s", 0), own.at[:, half, col, 1 - core], sibling)
        links.arrived(("own_sy", 0), own.at[:, 1 - half, col, 1 - core], sibling)
        for by in others:
            src_col = col_down(by)
            links.arrived(("own_sx", by), own.at[:, half, src_col, 1 - core], sibling)
            if split:
                piece = own.at[a_part, 1 - half, src_col, 1 - core]
                links.arrived(("own_sa", by), piece, sibling)
            if split < nq:
                piece = own.at[b_part, 1 - half, src_col, 1 - core]
                links.arrived(("own_sb", by), piece, sibling)
        for q in range(nq):
            block_copies[q].wait()

            def mirrored(n, carry, q=q):
                product = lax.dot_general(
                    blocks[q, :, tile_at(n)],
                    own[q].reshape(patches, width),
                    (((0,), (0,)), ((), ())),
                    preferred_element_type=F32,
                )
                mr[q, n // 2, pl.ds((n % 2) * per_tile, per_tile)] = product.reshape(
                    per_tile, 2, slice_rows, width
                )
                return carry

            lax.fori_loop(0, tiles, mirrored, 0)
            links.send(("ms", q), mr.at[q, :, :, 1 - core], ms.at[q], sibling)

    def unite():
        for i in range(slots):
            if i < nq:
                links.arrived(("ms", i), ms.at[i], sibling)
            if i == 0:

                @pl.when(core == 0)
                def _():
                    un[0] = mr[0, :, :, 0]

                @pl.when(core == 1)
                def _():
                    un[0] = ms[0]
            elif i == nq:

                @pl.when(core == 0)
                def _():
                    un[nq] = ms[nq - 1]

                @pl.when(core == 1)
                def _():
                    un[nq] = mr[nq - 1, :, :, 1]
            else:
                un[i] = mr[i - core, :, :, core] + ms[i - 1 + core]

    def sums_send(part):
        flip, piece_rows = sum_parts[part]
        side = halves[flip]
        for by in others:
            src = un.at[:, side, col_up(by), piece_rows]
            links.send(("mx", by, part), src, mx.at[by - 1, :, side, piece_rows], me_col[by])

    def opposite_pass():
        for side in range(2):
            piece = rf.at[:, side, core]
            links.arrived(("rf", 0), piece, sibling, side)
            links.send(("rf_s", 0), piece, piece, sibling, side)

    def window_pass():
        for by in others:
            src_col = col_down(by)
            for flip in range(2):
                piece = win.at[:, halves[flip], src_col, core]
                links.arrived(("win_x", by, flip), piece, sibling)
            piece = win.at[pl.ds(1 - core, nq), :, src_col, core]
            links.send(("win_s", by), piece, piece, sibling)

    def forward():
        for made in win_copies[1:]:
            made.wait()
        for by in range(columns):
            piece = win.at[pl.ds(core, nq), :, col_down(by), 1 - core]
            links.arrived(("win_s", by), piece, sibling)
        for q in QORDER:

            def forwarded(n, carry, q=q):
                product = jnp.dot(
                    blocks[q, tile_at(n), :],
                    win[core + q].reshape(patches, width),
                    preferred_element_type=F32,
                )
                fw[q, n // 2, pl.ds((n % 2) * per_tile, per_tile)] = product.reshape(
                    per_tile, 2, slice_rows, width
                )
                return carry

            lax.fori_loop(0, tiles, forwarded, 0)
            links.send(("fs", q), fw.at[q, :, :, 1 - core], fs.at[q], sibling)

    def forward_unite(q):
        links.arrived(("fs", q), fs.at[q], sibling)
        fw[q, :, :, core] = fw[q, :, :, core] + fs[q]

        @pl.when((half == 0) & (2 * col <= q))
        def _():
            fw[q, :, :, core] = fw[q, :, :, core] + un[q - 2 * col]

        if q not in XFIRST:
            links.send(("fy", q), fw.at[q, 1 - half, :, core], fy.at[q], partner)

    def opposite(q):
        if q == QORDER[0]:
            for side in range(2):
                far_copies[side].wait()
                links.arrived(("rf_s", 0), rf.at[:, side, 1 - core], sibling, side)
                for by in others:
                    links.arrived(("far", by, side), fbuf.at[side, :, col_down(by)], sibling)
        depth = 2 * slice_rows
        product = sum(
            jnp.dot(
                fbuf[side, q].reshape(columns * slice_rows, depth),
                rf[q, side].reshape(depth, width),
                preferred_element_type=F32,
            )
            for side in range(2)
        )
        fw[q, half, :, core] = fw[q, half, :, core] + product.reshape(columns, slice_rows, width)
        if q in XFIRST:
            for by in others:
                links.send(("fx", by, q), fw.at[q, :, col_up(by), core], fx.at[by - 1, q], me_col[by])

    def forward_pass(q):
        if q in XFIRST:
            total = fw[q, :, col, core]
            for by in others:
                links.arrived(("fx", by, q), fx.at[by - 1, q], sibling)
                total = total + fx[by - 1, q]
            fw[q, :, col, core] = total
            links.send(("fy", q), fw.at[q, 1 - half, col, core], fy.at[q, 0], partner)
        else:
            links.arrived(("fy", q), fy.at[q], partner)
            fw[q, half, :, core] = fw[q, half, :, core] + fy[q]
            for by in others:
                links.send(
                    ("fx", by, q),
                    fw.at[q, half, col_up(by), core],
                    fx.at[by - 1, q, half],
                    me_col[by],
                )

    def forward_end(q):
        if q in XFIRST:
            links.arrived(("fy", q), fy.at[q, 0], partner)
            out[q] = fw[q, half, col, core] + fy[q, 0]
        else:
            total = fw[q, half, col, core]
            for by in others:
                links.arrived(("fx", by, q), fx.at[by - 1, q, half], sibling)
                total = total + fx[by - 1, q, half]
            out[q] = total

    def sums_pass(part):
        flip, piece_rows = sum_parts[part]
        side = halves[flip]
        hz_own[:, side, piece_rows] = jnp.zeros((groups, part_rows, width), F32)
        hz_own[pl.ds(2 * col, slots), side, piece_rows] = un[:, side, col, piece_rows]
        for by in others:
            links.arrived(("mx", by, part), mx.at[by - 1, :, side, piece_rows], sibling)
            reach = pl.ds(2 * col_down(by), slots)
            hz_own[reach, side, piece_rows] = (
                hz_own[reach, side, piece_rows] + mx[by - 1, :, side, piece_rows]
            )
        for g, (first, count) in enumerate(parts):
            src = hz_own.at[pl.ds(first, count), side, piece_rows]
            dst = hz.at[half, pl.ds(first, count), piece_rows]
            target = at(row_up(start_of(half) + g), side, col, core)
            remote = links.copy(("hz", g, part), src, dst, target)
            if g == 0:
                conditional.append(remote)

                @pl.when(half == 1)
                def _(remote=remote):
                    remote.start()
            else:
                remote.start()

    scope = locals()
    for step in ORDER:
        name, *args = step.split()
        scope[name](*map(int, args))

    kinds, bands = tab.shape
    reflect_of = jnp.concatenate([tab[...]] * (width // bands), axis=1)
    across = lax.broadcasted_iota(jnp.int32, (slice_rows, slice_rows), 1)
    down = lax.broadcasted_iota(jnp.int32, (slice_rows, slice_rows), 0)

    def upright(values):
        spread = jnp.broadcast_to(values, (slice_rows, slice_rows))
        return jnp.sum(jnp.where(across == down, spread, 0), axis=1, keepdims=True)

    for q in range(nq):
        kind = upright(mat[pl.ds(q, 1), :])
        reflect = jnp.zeros((slice_rows, width), F32)
        for m in range(kinds):
            reflect = jnp.where(kind == m, reflect_of[m : m + 1, :], reflect)
        refl[q] = reflect
    emi_copy.wait()
    for q in range(nq):
        forward_end(q)
    for part, (flip, piece_rows) in enumerate(sum_parts):
        for g, (first, count) in enumerate(parts):
            piece = hz.at[halves[flip], pl.ds(first, count), piece_rows]
            if g == 0:

                @pl.when(halves[flip] == 1)
                def _(piece=piece, part=part):
                    links.arrived(("hz", 0, part), piece, sibling)
            else:
                links.arrived(("hz", g, part), piece, sibling)
    for q in range(nq):
        total = out[q]
        for half_from in range(2):
            for u in range(q + (0 if half_from else nq), groups, nq):
                total = total + hz[half_from, u]
        irradiation = total / upright(area[pl.ds(q, 1), :])
        out[q] = emi_v[q].astype(F32) + refl[q] * irradiation

    for made in links.sent:
        if any(made is other for other in conditional):

            @pl.when(half == 1)
            def _(made=made):
                made.wait_send()
        else:
            made.wait_send()


def on_device(rows, columns, radiosity, emission, areas, patch_material, reflect_table, pair_blocks, far_blocks):
    nq, slice_rows, width = radiosity.shape
    patches = pair_blocks.shape[2]
    slots = nq + 1
    groups = 2 * columns + nq - 1
    bf16 = jnp.bfloat16
    scratch = [
        pltpu.VMEM((nq, patches, patches), bf16),
        pltpu.VMEM((nq, 2, columns, 2, slice_rows, width), bf16),
        pltpu.VMEM((slots, 2, columns, 2, slice_rows, width), bf16),
        pltpu.VMEM((groups, 2, slice_rows, width), bf16),
        pltpu.VMEM((2, nq, columns, slice_rows, 2 * slice_rows), bf16),
        pltpu.VMEM((nq, 2, 2, slice_rows, width), bf16),
        pltpu.VMEM((nq, 2, columns, 2, slice_rows, width), F32),
        pltpu.VMEM((nq, 2, columns, slice_rows, width), F32),
        pltpu.VMEM((nq, columns, slice_rows, width), F32),
        pltpu.VMEM((columns - 1, nq, 2, slice_rows, width), F32),
        pltpu.VMEM((nq, 2, columns, 2, slice_rows, width), F32),
        pltpu.VMEM((nq, 2, columns, slice_rows, width), F32),
        pltpu.VMEM((slots, 2, columns, slice_rows, width), F32),
        pltpu.VMEM((columns - 1, slots, 2, slice_rows, width), F32),
        pltpu.VMEM((groups, 2, slice_rows, width), F32),
        pltpu.VMEM((2, groups, slice_rows, width), F32),
        pltpu.VMEM((nq, slice_rows, width), bf16),
        pltpu.VMEM((nq, slice_rows, width), F32),
        pltpu.SemaphoreType.DMA((160,)),
        pltpu.SemaphoreType.DMA((160,)),
        pltpu.SemaphoreType.DMA((16,)),
    ]
    any_space = pl.BlockSpec(memory_space=pl.ANY)
    vmem = pl.BlockSpec(memory_space=pltpu.VMEM)
    flops = 4 * nq * patches * patches * width
    return pl.pallas_call(
        functools.partial(kernel, rows, columns),
        out_shape=jax.ShapeDtypeStruct((nq, slice_rows, width), F32),
        in_specs=[any_space, any_space, vmem, vmem, vmem, any_space, any_space],
        out_specs=vmem,
        scratch_shapes=scratch,
        compiler_params=pltpu.CompilerParams(
            collective_id=0, has_side_effects=True, vmem_limit_bytes=58 * 2**20
        ),
        cost_estimate=pl.CostEstimate(
            flops=flops, bytes_accessed=2 * nq * patches * patches, transcendentals=0
        ),
    )(radiosity, emission, areas, patch_material, reflect_table, pair_blocks, far_blocks)


def solution(mesh):
    rows, stops = mesh.shape["row"], mesh.shape["stop"]
    return jax.shard_map(
        functools.partial(on_device, rows, stops // 4),
        mesh=mesh,
        in_specs=(
            P("row", "stop", None),
            P("row", "stop", None),
            P("row", "stop"),
            P("row", "stop"),
            P(),
            P("row", "stop", None, None),
            P("row", "stop", None),
        ),
        out_specs=P("row", "stop", None),
        check_vma=False,
    )
```

time: 633 us -> 92.5 us (0.15)
  waiting for transfers between devices: 551 us -> 0 us
  Pallas kernels: 0 us -> 90.6 us
  local copies, waits for them, and re-layouts: 26.1 us -> 1.67 us
  starting transfers between devices: 16.6 us -> 0 us
  matrix products: 15.1 us -> 0 us
  between operations: 14.3 us -> 0.01 us
  other arithmetic: 9.35 us -> 0 us
    ppermute x8 -> x0, waiting for transfers between devices: 349 us -> none  [shifted(): lax.ppermute(shard, axis, [(i, (i + by) % peers) for i in range(peers)])]
    unnamed x3 -> x0, waiting for transfers between devices: 148 us -> none
    pallas_call x0 -> x1, Pallas kernels: none -> 90.6 us  [on_device(): pl.pallas_call(functools.partial(kernel, rows, columns), out_shape=jax.Sh...]
    all_gather x1 -> x0, waiting for transfers between devices: 54.5 us -> none  [on_device(): own_rows = lax.all_gather(radiosity, 'stop', axis=1, tiled=True)]
    ppermute x8 -> x0, starting transfers between devices: 16.6 us -> none  [shifted(): lax.ppermute(shard, axis, [(i, (i + by) % peers) for i in range(peers)])]
    dot_general x4 -> x0, matrix products: 15.1 us -> none  [the longest x1 9.27 us: on_device(): jnp.einsum('qij,qjc->qic', blocks, window, preferred_element_type=jnp.flo...]
    broadcast_in_dim x1 -> x0, local copies, waits for them, and re-layouts: 9.94 us -> none  [on_device(): jnp.zeros(((reach + 1) * per_row,) + mirrored.shape[1:], jnp.float32)]
    add x3 -> x0, other arithmetic: 9.35 us -> none  [on_device(): shifted(carried, 'row', 1) + holder[step * per_row:(step + 1) * per_row]]
  transfers between devices with their start and end apart: 10 -> 0, of which waited for: 8 -> 0; matrix products, arithmetic and copies ran while one was open for 1% -> 0% of each run, Pallas kernels for 0% -> 0%
where the time goes in v2:
time: 92.5 us; the launch traced here: 92.3 us
  Pallas kernels  90.6 us (98%)
  local copies, waits for them, and re-layouts  1.67 us (2%)
    pallas_call x1, Pallas kernels, on_device(): pl.pallas_call(functools.partial(kernel, rows, columns), out_shape=jax.Sh...  90.6 us

profile of v2, /device:TPU:1, one launch (start us, length us, event | category | flops | bytes accessed | tf_op | source)
XLA Modules:
  0.0 92.3 jit_solution(9359658998788396202)
XLA Ops:
  0.0 90.6 %shard_map.73 = f32[4,64,256]{2,1,0:T(8,128)} custom-call(bf16[4,64,256]{2,1,0:T(8,128)(2,1)} %rad.1, bf16[4,64,256]{2,1,0:T(8,128)(2,1)} %emi.1, f32[4,64]{1,0:T(4,128)} %area.1, s32[4,64]{1,0:T(4,128)} %mat.1, f32[16,32]{1,0:T(8,128)} %tab.1, bf16[4,1,1024,1024]{3,2,1,0:T(8,128)(2,1)} %pair.1, bf16[4,64,1024]{2,1,0:T(8,128)(2,1)} %far.1), custom_call_target="tpu_custom_call" | custom-call | flops 4294967296 | bytes 8388608 | tf_op jit(solution)/shard_map/pallas_call | solution.py:575
  90.6 1.7 %copy.9 = f32[4,64,256]{2,1,0:T(8,128)} copy(f32[4,64,256]{2,1,0:T(8,128)} %shard_map.73) | data formatting | bytes 524288

commit v3 on v2

--- a/solution.py
+++ b/solution.py
@@ -18,13 +18,17 @@
     "own_send",
     "reach_send 0",
     "reach_send 1",
+    "reach_send 2",
+    "reach_send 3",
     "own_pass_y",
     "own_pass_x",
     "reach_pass 0",
+    "reach_pass 1",
     "own_end",
-    "reach_pass 1",
+    "reach_pass 2",
+    "mirror",
+    "reach_pass 3",
     "opposite_send",
-    "mirror",
     "unite",
     "opposite_pass",
     "window_pass",
@@ -133,11 +137,11 @@
     for by in others:
         for key in ("own_x", "own_sx", "own_ya", "own_xb", "own_sa", "own_sb"):
             links.name((key, by))
-        for flip in range(2):
-            links.name(("far", by, flip))
-            links.name(("win_x", by, flip))
+        for side in range(2):
+            links.name(("far", by, side))
         for part in range(4):
             links.name(("mx", by, part))
+            links.name(("win_x", by, part))
         for q in range(nq):
             links.name(("fx", by, q))
     for by in range(columns):
@@ -147,10 +151,9 @@
     for key in ("rf", "rf_s"):
         links.name((key, 0), 2)
     for g in range(len(parts)):
-        for flip in range(2):
-            links.name(("grp", g, flip))
         for part in range(4):
             links.name(("hz", g, part))
+            links.name(("grp", g, part))
     for q in range(nq):
         for key in ("ms", "fs", "fy"):
             links.name((key, q))
@@ -199,13 +202,15 @@
     pl.semaphore_wait(barrier, len(peers))
 
     mine = own.at[:, half, col, core]
-    win_copies, conditional = [], []
+    win_copies, near_copies, conditional = [], [], []
     a_part, b_part = pl.ds(0, split), pl.ds(split, nq - split)
-    per_tile = columns // 2
+    per_tile = columns
     tile = per_tile * 2 * slice_rows
     tiles = patches // tile
     part_rows = slice_rows // 2
-    sum_parts = [(flip, pl.ds(n * part_rows, part_rows)) for flip in (1, 0) for n in range(2)]
+    row_parts = [pl.ds(n * part_rows, part_rows) for n in range(2)]
+    sum_parts = [(flip, piece_rows) for flip in (1, 0) for piece_rows in row_parts]
+    reach_parts = [(flip, piece_rows) for flip in (0, 1) for piece_rows in row_parts]
 
     def tile_at(n):
         return pl.ds(pl.multiple_of(n * tile, tile), tile)
@@ -216,16 +221,18 @@
             links.send(("own_x", by), rad, mine, me_col[by])
         links.send(("own_s", 0), rad, mine, sibling)
 
-    def reach_send(flip):
+    def reach_send(part):
+        flip, piece_rows = reach_parts[part]
         for g, (first, count) in enumerate(parts):
-            src = rad.at[pl.ds(0, count)]
-            dst = grp.at[pl.ds(first, count), half]
+            src = rad.at[pl.ds(0, count), piece_rows]
+            dst = grp.at[pl.ds(first, count), half, piece_rows]
             source_row = row_down(start_of(halves[flip]) + g)
-            remote = links.copy(("grp", g, flip), src, dst, at(source_row, halves[flip], col, core))
+            target = at(source_row, halves[flip], col, core)
+            remote = links.copy(("grp", g, part), src, dst, target)
             if g == 0 and flip == 0:
                 near = local(src, dst)
                 conditional.append(remote)
-                win_copies.append(near)
+                near_copies.append(near)
 
                 @pl.when(half == 1)
                 def _(remote=remote):
@@ -277,28 +284,31 @@
                 links.arrived(("own_ya", by), piece, partner)
                 links.send(("own_sa", by), piece, piece, sibling)
 
-    def reach_pass(flip):
+    def reach_pass(part):
+        flip, piece_rows = reach_parts[part]
         side = halves[flip]
         for g, (first, count) in enumerate(parts):
-            piece = grp.at[pl.ds(first, count), side]
+            piece = grp.at[pl.ds(first, count), side, piece_rows]
             if g == 0 and flip == 0:
+                near = near_copies[part]
 
                 @pl.when(half == 1)
                 def _(piece=piece):
-                    links.arrived(("grp", 0, 0), piece, sibling)
+                    links.arrived(("grp", 0, part), piece, sibling)
 
                 @pl.when(half == 0)
                 def _():
-                    win_copies[0].wait()
+                    near.wait()
             else:
-                links.arrived(("grp", g, flip), piece, sibling)
-        for by in others:
-            src = grp.at[pl.ds(2 * col_up(by), slots), side]
-            links.send(("win_x", by, flip), src, win.at[:, side, col, core], me_col[by])
-        made = local(grp.at[pl.ds(2 * col, slots), side], win.at[:, side, col, core])
+                links.arrived(("grp", g, part), piece, sibling)
+        dst = win.at[:, side, col, core, piece_rows]
+        for by in others:
+            src = grp.at[pl.ds(2 * col_up(by), slots), side, piece_rows]
+            links.send(("win_x", by, part), src, dst, me_col[by])
+        made = local(grp.at[pl.ds(2 * col, slots), side, piece_rows], dst)
         made.start()
         win_copies.append(made)
-        if flip == 1:
+        if part == 3:
             src = grp.at[pl.ds(2 * col + 1 - core, nq)]
             links.send(("win_s", 0), src, win.at[pl.ds(1 - core, nq), :, col, core], sibling)
 
@@ -325,12 +335,12 @@
                     (((0,), (0,)), ((), ())),
                     preferred_element_type=F32,
                 )
-                mr[q, n // 2, pl.ds((n % 2) * per_tile, per_tile)] = product.reshape(
+                mr[q, n] = product.reshape(
                     per_tile, 2, slice_rows, width
                 )
                 return carry
 
-            lax.fori_loop(0, tiles, mirrored, 0)
+            lax.fori_loop(0, tiles, mirrored, 0, unroll=True)
             links.send(("ms", q), mr.at[q, :, :, 1 - core], ms.at[q], sibling)
 
     def unite():
@@ -374,14 +384,14 @@
     def window_pass():
         for by in others:
             src_col = col_down(by)
-            for flip in range(2):
-                piece = win.at[:, halves[flip], src_col, core]
-                links.arrived(("win_x", by, flip), piece, sibling)
+            for part, (flip, piece_rows) in enumerate(reach_parts):
+                piece = win.at[:, halves[flip], src_col, core, piece_rows]
+                links.arrived(("win_x", by, part), piece, sibling)
             piece = win.at[pl.ds(1 - core, nq), :, src_col, core]
             links.send(("win_s", by), piece, piece, sibling)
 
     def forward():
-        for made in win_copies[1:]:
+        for made in win_copies:
             made.wait()
         for by in range(columns):
             piece = win.at[pl.ds(core, nq), :, col_down(by), 1 - core]
@@ -394,12 +404,12 @@
                     win[core + q].reshape(patches, width),
                     preferred_element_type=F32,
                 )
-                fw[q, n // 2, pl.ds((n % 2) * per_tile, per_tile)] = product.reshape(
+                fw[q, n] = product.reshape(
                     per_tile, 2, slice_rows, width
                 )
                 return carry
 
-            lax.fori_loop(0, tiles, forwarded, 0)
+            lax.fori_loop(0, tiles, forwarded, 0, unroll=True)
             links.send(("fs", q), fw.at[q, :, :, 1 - core], fs.at[q], sibling)
 
     def forward_unite(q):
@@ -567,7 +577,7 @@
         pltpu.VMEM((nq, slice_rows, width), F32),
         pltpu.SemaphoreType.DMA((160,)),
         pltpu.SemaphoreType.DMA((160,)),
-        pltpu.SemaphoreType.DMA((16,)),
+        pltpu.SemaphoreType.DMA((24,)),
     ]
     any_space = pl.BlockSpec(memory_space=pl.ANY)
     vmem = pl.BlockSpec(memory_space=pltpu.VMEM)

time: 92.5 us -> 89.1 us (0.963)
  Pallas kernels: 90.6 us -> 87.3 us
    pallas_call x1, Pallas kernels: 90.6 us -> 87.3 us  [on_device(): pl.pallas_call(functools.partial(kernel, rows, columns), out_shape=jax.Sh...]
where the time goes in v3:
time: 89.1 us; the launch traced here: 88.9 us
  Pallas kernels  87.3 us (98%)
  local copies, waits for them, and re-layouts  1.67 us (2%)
    pallas_call x1, Pallas kernels, on_device(): pl.pallas_call(functools.partial(kernel, rows, columns), out_shape=jax.Sh...  87.3 us

profile of v3, /device:TPU:1, one launch (start us, length us, event | category | flops | bytes accessed | tf_op | source)
XLA Modules:
  0.0 88.9 jit_solution(6558727344755220399)
XLA Ops:
  0.0 87.3 %shard_map.73 = f32[4,64,256]{2,1,0:T(8,128)} custom-call(bf16[4,64,256]{2,1,0:T(8,128)(2,1)} %rad.1, bf16[4,64,256]{2,1,0:T(8,128)(2,1)} %emi.1, f32[4,64]{1,0:T(4,128)} %area.1, s32[4,64]{1,0:T(4,128)} %mat.1, f32[16,32]{1,0:T(8,128)} %tab.1, bf16[4,1,1024,1024]{3,2,1,0:T(8,128)(2,1)} %pair.1, bf16[4,64,1024]{2,1,0:T(8,128)(2,1)} %far.1), custom_call_target="tpu_custom_call" | custom-call | flops 4294967296 | bytes 8388608 | tf_op jit(solution)/shard_map/pallas_call | solution.py:585
  87.3 1.7 %copy.9 = f32[4,64,256]{2,1,0:T(8,128)} copy(f32[4,64,256]{2,1,0:T(8,128)} %shard_map.73) | data formatting | bytes 524288

commit v4 on v3

--- a/solution.py
+++ b/solution.py
@@ -13,7 +13,6 @@
 
 SPLIT = 0
 XFIRST = ()
-QORDER = (0, 1, 2, 3)
 ORDER = (
     "own_send",
     "reach_send 0",
@@ -36,10 +35,12 @@
     "sums_send 1",
     "far_send",
     "sums_send 2",
-    "sums_send 3",
-    "forward",
+    "forward 0",
+    "forward 1",
     "forward_unite 0",
+    "forward 2",
     "forward_unite 1",
+    "forward 3",
     "forward_unite 2",
     "forward_unite 3",
     "opposite 0",
@@ -47,6 +48,7 @@
     "opposite 2",
     "opposite 3",
     "sums_pass 0",
+    "sums_send 3",
     "forward_pass 0",
     "sums_pass 1",
     "forward_pass 1",
@@ -94,8 +96,9 @@
 
 def kernel(
     rows, columns,
-    rad, emi, area, mat, tab, pair, far, out,
+    rad, emi, area_in, mat_in, tab_in, pair, far, result,
     blocks, own, win, grp, fbuf, rf, fw, fs, fy, fx, mr, ms, un, mx, hz_own, hz, emi_v, refl,
+    area, mat, tab, out,
     send_sem, recv_sem, local_sem,
 ):
     nq, slice_rows, width = rad.shape
@@ -197,8 +200,11 @@
         made = local(far.at[:, :, far_columns(side, col)], fbuf.at[side, :, col])
         made.start()
         far_copies.append(made)
-    emi_copy = local(emi, emi_v)
-    emi_copy.start()
+    small_copies = []
+    for src, dst in ((emi, emi_v), (area_in, area), (mat_in, mat), (tab_in, tab)):
+        made = local(src, dst)
+        made.start()
+        small_copies.append(made)
     pl.semaphore_wait(barrier, len(peers))
 
     mine = own.at[:, half, col, core]
@@ -390,27 +396,25 @@
             piece = win.at[pl.ds(1 - core, nq), :, src_col, core]
             links.send(("win_s", by), piece, piece, sibling)
 
-    def forward():
-        for made in win_copies:
-            made.wait()
-        for by in range(columns):
-            piece = win.at[pl.ds(core, nq), :, col_down(by), 1 - core]
-            links.arrived(("win_s", by), piece, sibling)
-        for q in QORDER:
-
-            def forwarded(n, carry, q=q):
-                product = jnp.dot(
-                    blocks[q, tile_at(n), :],
-                    win[core + q].reshape(patches, width),
-                    preferred_element_type=F32,
-                )
-                fw[q, n] = product.reshape(
-                    per_tile, 2, slice_rows, width
-                )
-                return carry
-
-            lax.fori_loop(0, tiles, forwarded, 0, unroll=True)
-            links.send(("fs", q), fw.at[q, :, :, 1 - core], fs.at[q], sibling)
+    def forward(q):
+        if q == 0:
+            for made in win_copies:
+                made.wait()
+            for by in range(columns):
+                piece = win.at[pl.ds(core, nq), :, col_down(by), 1 - core]
+                links.arrived(("win_s", by), piece, sibling)
+
+        def forwarded(n, carry):
+            product = jnp.dot(
+                blocks[q, tile_at(n), :],
+                win[core + q].reshape(patches, width),
+                preferred_element_type=F32,
+            )
+            fw[q, n] = product.reshape(per_tile, 2, slice_rows, width)
+            return carry
+
+        lax.fori_loop(0, tiles, forwarded, 0, unroll=True)
+        links.send(("fs", q), fw.at[q, :, :, 1 - core], fs.at[q], sibling)
 
     def forward_unite(q):
         links.arrived(("fs", q), fs.at[q], sibling)
@@ -424,7 +428,7 @@
             links.send(("fy", q), fw.at[q, 1 - half, :, core], fy.at[q], partner)
 
     def opposite(q):
-        if q == QORDER[0]:
+        if q == 0:
             for side in range(2):
                 far_copies[side].wait()
                 links.arrived(("rf_s", 0), rf.at[:, side, 1 - core], sibling, side)
@@ -504,6 +508,8 @@
         name, *args = step.split()
         scope[name](*map(int, args))
 
+    for made in small_copies:
+        made.wait()
     kinds, bands = tab.shape
     reflect_of = jnp.concatenate([tab[...]] * (width // bands), axis=1)
     across = lax.broadcasted_iota(jnp.int32, (slice_rows, slice_rows), 1)
@@ -519,7 +525,19 @@
         for m in range(kinds):
             reflect = jnp.where(kind == m, reflect_of[m : m + 1, :], reflect)
         refl[q] = reflect
-    emi_copy.wait()
+
+    def sends_end(some):
+        for made in some:
+            if any(made is other for other in conditional):
+
+                @pl.when(half == 1)
+                def _(made=made):
+                    made.wait_send()
+            else:
+                made.wait_send()
+
+    late = len(others) + len(parts)
+    sends_end(links.sent[:-late])
     for q in range(nq):
         forward_end(q)
     for part, (flip, piece_rows) in enumerate(sum_parts):
@@ -532,6 +550,7 @@
                     links.arrived(("hz", 0, part), piece, sibling)
             else:
                 links.arrived(("hz", g, part), piece, sibling)
+    result_copies = []
     for q in range(nq):
         total = out[q]
         for half_from in range(2):
@@ -539,15 +558,12 @@
                 total = total + hz[half_from, u]
         irradiation = total / upright(area[pl.ds(q, 1), :])
         out[q] = emi_v[q].astype(F32) + refl[q] * irradiation
-
-    for made in links.sent:
-        if any(made is other for other in conditional):
-
-            @pl.when(half == 1)
-            def _(made=made):
-                made.wait_send()
-        else:
-            made.wait_send()
+        made = local(out.at[q], result.at[q])
+        made.start()
+        result_copies.append(made)
+    sends_end(links.sent[-late:])
+    for made in result_copies:
+        made.wait()
 
 
 def on_device(rows, columns, radiosity, emission, areas, patch_material, reflect_table, pair_blocks, far_blocks):
@@ -575,18 +591,21 @@
         pltpu.VMEM((2, groups, slice_rows, width), F32),
         pltpu.VMEM((nq, slice_rows, width), bf16),
         pltpu.VMEM((nq, slice_rows, width), F32),
+        pltpu.VMEM(areas.shape, F32),
+        pltpu.VMEM(patch_material.shape, jnp.int32),
+        pltpu.VMEM(reflect_table.shape, F32),
+        pltpu.VMEM((nq, slice_rows, width), F32),
         pltpu.SemaphoreType.DMA((160,)),
         pltpu.SemaphoreType.DMA((160,)),
         pltpu.SemaphoreType.DMA((24,)),
     ]
     any_space = pl.BlockSpec(memory_space=pl.ANY)
-    vmem = pl.BlockSpec(memory_space=pltpu.VMEM)
     flops = 4 * nq * patches * patches * width
     return pl.pallas_call(
         functools.partial(kernel, rows, columns),
         out_shape=jax.ShapeDtypeStruct((nq, slice_rows, width), F32),
-        in_specs=[any_space, any_space, vmem, vmem, vmem, any_space, any_space],
-        out_specs=vmem,
+        in_specs=[any_space] * 7,
+        out_specs=any_space,
         scratch_shapes=scratch,
         compiler_params=pltpu.CompilerParams(
             collective_id=0, has_side_effects=True, vmem_limit_bytes=58 * 2**20

time: 89.1 us -> 87.4 us (0.981)
  Pallas kernels: 87.3 us -> 84.9 us
    pallas_call x1, Pallas kernels: 87.3 us -> 84.9 us  [on_device(): pl.pallas_call(functools.partial(kernel, rows, columns), out_shape=jax.Sh...]
where the time goes in v4:
time: 87.4 us; the launch traced here: 86.5 us
  Pallas kernels  84.9 us (97%)
  local copies, waits for them, and re-layouts  1.67 us (2%)
    pallas_call x1, Pallas kernels, on_device(): pl.pallas_call(functools.partial(kernel, rows, columns), out_shape=jax.Sh...  84.9 us

profile of v4, /device:TPU:1, one launch (start us, length us, event | category | flops | bytes accessed | tf_op | source)
XLA Modules:
  0.0 86.5 jit_solution(16945867697820023064)
XLA Ops:
  0.0 84.9 %shard_map.73 = f32[4,64,256]{2,1,0:T(8,128)} custom-call(bf16[4,64,256]{2,1,0:T(8,128)(2,1)} %rad.1, bf16[4,64,256]{2,1,0:T(8,128)(2,1)} %emi.1, f32[4,64]{1,0:T(4,128)} %area_in.1, s32[4,64]{1,0:T(4,128)} %mat_in.1, f32[16,32]{1,0:T(8,128)} %tab_in.1, bf16[4,1,1024,1024]{3,2,1,0:T(8,128)(2,1)} %pair.1, bf16[4,64,1024]{2,1,0:T(8,128)(2,1)} %far.1), custom_call_target="tpu_custom_call" | custom-call | flops 4294967296 | bytes 8388608 | tf_op jit(solution)/shard_map/pallas_call | solution.py:604
  84.9 1.7 %copy.9 = f32[4,64,256]{2,1,0:T(8,128)} copy(f32[4,64,256]{2,1,0:T(8,128)} %shard_map.73) | data formatting | bytes 524288

commit v5 on v4

--- a/solution.py
+++ b/solution.py
@@ -43,12 +43,12 @@
     "forward 3",
     "forward_unite 2",
     "forward_unite 3",
+    "sums_pass 0",
+    "sums_send 3",
     "opposite 0",
     "opposite 1",
     "opposite 2",
     "opposite 3",
-    "sums_pass 0",
-    "sums_send 3",
     "forward_pass 0",
     "sums_pass 1",
     "forward_pass 1",

time: 87.4 us -> 87.4 us (level)
  no operation moved by 1% of the time
where the time goes in v5:
time: 87.4 us; the launch traced here: 86.5 us
  Pallas kernels  84.9 us (97%)
  local copies, waits for them, and re-layouts  1.67 us (2%)
    pallas_call x1, Pallas kernels, on_device(): pl.pallas_call(functools.partial(kernel, rows, columns), out_shape=jax.Sh...  84.9 us

profile of v5, /device:TPU:1, one launch (start us, length us, event | category | flops | bytes accessed | tf_op | source)
XLA Modules:
  0.0 86.5 jit_solution(2240875277562830229)
XLA Ops:
  0.0 84.9 %shard_map.73 = f32[4,64,256]{2,1,0:T(8,128)} custom-call(bf16[4,64,256]{2,1,0:T(8,128)(2,1)} %rad.1, bf16[4,64,256]{2,1,0:T(8,128)(2,1)} %emi.1, f32[4,64]{1,0:T(4,128)} %area_in.1, s32[4,64]{1,0:T(4,128)} %mat_in.1, f32[16,32]{1,0:T(8,128)} %tab_in.1, bf16[4,1,1024,1024]{3,2,1,0:T(8,128)(2,1)} %pair.1, bf16[4,64,1024]{2,1,0:T(8,128)(2,1)} %far.1), custom_call_target="tpu_custom_call" | custom-call | flops 4294967296 | bytes 8388608 | tf_op jit(solution)/shard_map/pallas_call | solution.py:604
  84.9 1.7 %copy.9 = f32[4,64,256]{2,1,0:T(8,128)} copy(f32[4,64,256]{2,1,0:T(8,128)} %shard_map.73) | data formatting | bytes 524288
